TPU v7x, 128 devices: a whole 4x4x4 slice. The times are simulated.
128 devices in a mesh: win: 32 (over z, y, core), mlp: 4 (over x).
Axes of the slice: x: 4, y: 4, z: 4, core: 2. Of those that a mesh axis runs over, the one named last changes fastest.
Arguments:
- tokens_in: bfloat16 [150528, 384], P(('win', 'mlp')), may hold values from -6 to 6
- out_grad: bfloat16 [150528, 384], P(('win', 'mlp')), may hold values from -6 to 6
- window_live: int32 [3072], P(('win', 'mlp')), may hold values from 0 to 1, as said below
- region_ids: int32 [150528], P(('win', 'mlp')), may hold values from 0 to 4, as said below
- qkv_weight: float32 [384, 1152], replicated, may hold values from -0.3125 to 0.3125
- proj_weight: float32 [384, 384], replicated, may hold values from -0.875 to 0.875
- rel_table: float32 [169, 12], replicated, may hold values from -4 to 4
- small_params: float32 [3072], replicated, may hold values from -0.9 to 1.75
- fc1_weight: float32 [384, 1536], P(None, 'mlp'), may hold values from -0.3125 to 0.3125
- fc1_bias: float32 [1536], P('mlp'), may hold values from -1.2 to 1.2
- fc2_weight: float32 [1536, 384], P('mlp'), may hold values from -0.15625 to 0.15625
- qkv_row: float32 [384], replicated, as said below
- qkv_col: float32 [1152], replicated, as said below
- proj_row: float32 [384], replicated, as said below
- proj_col: float32 [384], replicated, as said below
- fc1_row: float32 [384], replicated, as said below
- fc1_col: float32 [1536], P('mlp'), as said below
- fc2_row: float32 [1536], P('mlp'), as said below
- fc2_col: float32 [384], replicated, as said below
- fc1_bias_state: float32 [1536], P('mlp'), as said below
- small_state: float32 [3072], replicated, as said below
- table_state: float32 [169, 12], replicated, as said below
Outputs:
- block_out: float32 [150528, 384], P(('win', 'mlp'))
- input_grad: float32 [150528, 384], P(('win', 'mlp'))
- qkv_grad: float32 [384, 1152], P(('win', 'mlp'))
- qkv_row_new: float32 [384], P(('win', 'mlp'))
- qkv_col_new: float32 [1152], replicated
- qkv_new: float32 [384, 1152], P(('win', 'mlp'))
- qkv_new_low: bfloat16 [384, 1152], P(('win', 'mlp'))
- proj_grad: float32 [384, 384], P(('win', 'mlp'))
- proj_row_new: float32 [384], P(('win', 'mlp'))
- proj_col_new: float32 [384], replicated
- proj_new: float32 [384, 384], P(('win', 'mlp'))
- proj_new_low: bfloat16 [384, 384], P(('win', 'mlp'))
- fc1_grad: float32 [384, 1536], P(None, 'mlp')
- fc1_row_new: float32 [384], replicated
- fc1_col_new: float32 [1536], P('mlp')
- fc1_new: float32 [384, 1536], P(None, 'mlp')
- fc1_new_low: bfloat16 [384, 1536], P(None, 'mlp')
- fc2_grad: float32 [1536, 384], P('mlp')
- fc2_row_new: float32 [1536], P('mlp')
- fc2_col_new: float32 [384], replicated
- fc2_new: float32 [1536, 384], P('mlp')
- fc2_new_low: bfloat16 [1536, 384], P('mlp')
- fc1_bias_grad: float32 [1536], P('mlp')
- fc1_bias_state_new: float32 [1536], P('mlp')
- fc1_bias_new: float32 [1536], P('mlp')
- small_grad: float32 [3072], replicated
- small_state_new: float32 [3072], replicated
- small_new: float32 [3072], replicated
- table_grad: float32 [169, 12], replicated
- table_state_new: float32 [169, 12], replicated
- table_new: float32 [169, 12], replicated
Inputs may be any that keep to these rules, and one draw needn't show every extreme that they name: `window_live`: on each device's 24 window slots the live ones come first; at least half of each device's slots are live, and in every draw some device has all 24 live. `region_ids`: ids split a window at row and at column 4. `qkv_row`: Positive. `qkv_col`: Positive. `proj_row`: Positive. `proj_col`: Positive. `fc1_row`: Positive. `fc1_col`: Positive. `fc2_row`: Positive. `fc2_col`: Positive. `fc1_bias_state`: Positive. `small_state`: Positive. `table_state`: Positive.
All inputs are finite; a program needn't handle non-finite values.
Results may differ from a plain program's by a relative error of at most 0.0095.
The roundings to bfloat16 on the way count: a program that leaves them out, or rounds other values in their place, can miss the bound.
Values may be sent and summed in bfloat16 or wider, within the bound.
A program may use at most 128 MiB of HBM per device.

v0:
```python
import functools
import math

import jax
import jax.numpy as jnp
from jax import lax
from jax.experimental import pallas as pl
from jax.experimental.pallas import tpu as pltpu
from jax.sharding import PartitionSpec as P

D = 384
FF = 1536
QKV = 3 * D
HEADS = 12
WIN = 7
SPAN = WIN * WIN
STEP = 10
DECAY = 1.0 - STEP ** (-0.8)
EPS_NORM = 1e-05
EPS_SQ = 1e-30
VEC_RATE = 0.3
SCALE = 32 ** (-0.5)
FAR = -1e30
LOG2E = math.log2(math.e)
FACTOR = (2.0 * math.pi) ** (-0.5)

PLACE = (0, 1, 3, 2)
GROUPS = 3
PER = 8
G_TOK = PER * SPAN
G_ROWS = 400
ROWS = GROUPS * G_ROWS
TOK = GROUPS * G_TOK
CHUNK = 64
KEYS = 56
SETS = 3
LANES = 4 * CHUNK

MESH = pl.DeviceIdType.MESH
F32 = jnp.float32
BF16 = jnp.bfloat16


def dot(a, b):
    return jnp.dot(a, b, preferred_element_type=F32)


def dot_nt(a, b):
    return lax.dot_general(a, b, (((1,), (1,)), ((), ())), preferred_element_type=F32)


def dot_tn(a, b):
    return lax.dot_general(a, b, (((0,), (0,)), ((), ())), preferred_element_type=F32)


def dot_exact(a, b):
    return jnp.dot(a, b, precision=lax.Precision.HIGHEST, preferred_element_type=F32)


def iota(shape, dim):
    return lax.broadcasted_iota(jnp.int32, shape, dim)


def fold_rows(x):
    total = x[0:8]
    for i in range(1, x.shape[0] // 8):
        total = total + x[8 * i : 8 * i + 8]
    return total


def row_mean(x):
    return jnp.sum(x, axis=1, keepdims=True) * (1.0 / D)


def normalize(x):
    center = x - row_mean(x)
    inverse = lax.rsqrt(row_mean(center * center) + EPS_NORM)
    return center * inverse, inverse


def normalize_back(u, gain, scaled, inverse):
    weighted = u * gain
    return inverse * (weighted - row_mean(weighted) - scaled * row_mean(weighted * scaled))


def gelu_parts(v):
    density = jnp.exp2((v * v) * (-0.5 * LOG2E) + math.log2(FACTOR))
    t = 1.0 / (1.0 + (0.3275911 * 0.5**0.5) * jnp.abs(v))
    c = 0.5 / FACTOR
    poly = (1.061405429 * c) * t - 1.453152027 * c
    poly = poly * t + 1.421413741 * c
    poly = poly * t - 0.284496736 * c
    poly = poly * t + 0.254829592 * c
    tail = density * (poly * t)
    phi = jnp.where(v < 0.0, tail, 1.0 - tail)
    return v * phi, phi + v * density


def barrel(x, amount, right):
    width = x.shape[1]
    for k in range(7):
        step = 1 << k
        moved = pltpu.roll(x, step if right else width - step, 1)
        x = jnp.where((amount & step) != 0, moved, x)
    return x


def embed(i):
    return 13 * (i // WIN) + i % WIN


def chunk_start(w):
    return pl.multiple_of((w // PER) * G_ROWS + (w % PER) * 48, 16)


def widen(tok, x_ref):
    for a in range(GROUPS):
        for r in range(0, G_TOK, 56):
            src = a * G_TOK + r
            low = src // 16 * 16
            x_ref[a * G_ROWS + r : a * G_ROWS + r + 56, :] = (
                tok[low : low + 64 if low + 64 <= TOK else TOK, :].astype(F32)[src - low : src - low + 56]
            )
        x_ref[a * G_ROWS + G_TOK : (a + 1) * G_ROWS, :] = jnp.zeros((G_ROWS - G_TOK, D), F32)


def prologue(region, table, emask, bias, mask):
    row = iota((LANES, 128), 0)
    lane = iota((LANES, 128), 1)
    for b in range(PER):
        i = row % CHUNK
        keep = (i >= b) & (i < b + SPAN) & (lane // 32 == row // CHUNK)
        emask[b] = jnp.where(keep, 1.0, 0.0).astype(BF16)
    j = iota((KEYS, 256), 0)
    amount = jnp.maximum(84 - embed(j), 0)
    jl = iota((KEYS, LANES), 0)
    il = iota((KEYS, LANES), 1) % CHUNK
    for g in range(SETS):
        base = jnp.zeros((KEYS, LANES), F32)
        for h in range(4):
            line = jnp.concatenate([table[4 * g + h : 4 * g + h + 1, :], jnp.zeros((1, 87), F32)], axis=1)
            wide = jnp.broadcast_to(line, (KEYS, 256))
            wide = barrel(wide, amount, False)[:, :128]
            lane_to = iota((128, LANES), 1) - CHUNK * h
            pick = (iota((128, LANES), 0) == embed(lane_to)) & (lane_to >= 0) & (lane_to < SPAN)
            base = base + dot_exact(wide, jnp.where(pick, 1.0, 0.0))
        for b in range(PER):
            moved = pltpu.roll(pltpu.roll(base, b, 0), b, 1) if b else base
            key_ok = (jl >= b) & (jl < b + SPAN)
            query_ok = (il >= b) & (il < b + SPAN)
            bias[b, g] = jnp.where(key_ok, jnp.where(query_ok, moved, 0.0), FAR)
    eye = iota((CHUNK, CHUNK), 0) == iota((CHUNK, CHUNK), 1)
    region_row = jnp.concatenate([region[...].reshape(1, TOK).astype(F32), jnp.zeros((1, 104), F32)], axis=1)
    for w in range(GROUPS * PER):
        start = (w // PER) * G_TOK + (w % PER) * 48
        line = region_row[:, start : start + CHUNK]
        column = jnp.sum(jnp.where(eye, jnp.broadcast_to(line, (CHUNK, CHUNK)), 0.0), axis=1, keepdims=True)
        wide = jnp.concatenate([line] * 4, axis=1)
        mask[w] = jnp.where(column[:KEYS] != wide, -100.0, 0.0)


def pad_keys(x):
    return jnp.concatenate([x, jnp.zeros((CHUNK - KEYS, x.shape[1]), x.dtype)], axis=0)


def spread(x, keep):
    return jnp.concatenate([x] * 4, axis=0) * keep


def collect(full):
    head = iota((CHUNK, 128), 1) // 32
    parts = [full[CHUNK * h : CHUNK * (h + 1)] for h in range(4)]
    low = jnp.where(head == 0, parts[0], parts[1])
    high = jnp.where(head == 2, parts[2], parts[3])
    return jnp.where(head < 2, low, high)


def packed(ref):
    at, views = 0, []
    for rows in (24, 16, 16, 32, 24, 8, 32, 16):
        views.append(ref.at[at : at + rows])
        at += rows
    return views


def block_kernel(
    live_windows, region, tok_in, og_in, wq_in, wp_in, fc1_in, fc2_in, table, small,
    fc1_b, fc1_state, fc1_col, fc2_row, qkv_row, proj_row,
    out_to, gin_to, fin_to, pack,
    x_ref, xh1, inv1, inv2, n1, n2, qkv, att_b, probs, back, hidden, ig, dqkv,
    emask, bias, mask, tacc, s1, s2, sums, b1_acc, wq_b, wp_b, w1, w2, tok, og, wq, wp, fc1, fc2, fin, fin_b, b1, stage, in_sem, out_sem,
    fcl, fr1, fr2, ft, fr3, fr4, fst, atl, ar1, ar2, ar3, ar4, ast, vx, vy, at_total,
    w_send, w_recv, b_send, b_recv, pair_send, pair_recv, f1s, f1r, f2s, f2r, f3s, f3r, f4s, f4r, f5s, f5r, f7s, f7r, f8s, f8r,
    a1s, a1r, a2s, a2r, a3s, a3r, a4s, a4r, a5s, a5r, vxs, vxr, vys, vyr,
):
    win, mlp = lax.axis_index("win"), lax.axis_index("mlp")
    vec, fc_sums, at_sums, own_g, own_wq, own_wp, b1_all, own_r = packed(pack)
    z, y, core = win // 8, (win // 2) % 4, win % 2
    pair = win + 1 - 2 * core

    def along_x(d):
        return win, (mlp + d) % 4

    def along_y(d):
        return z * 8 + ((y + d) % 4) * 2 + core, mlp

    def along_z(d):
        return ((z + d) % 4) * 8 + y * 2 + core, mlp

    def plane_peer(d):
        return ((z + d // 4) % 4) * 8 + ((y + d % 4) % 4) * 2 + core, mlp

    def class_peer(d):
        return pair if d >= 4 else win, (mlp + d) % 4

    loads = [
        pltpu.make_async_copy(src, dst, in_sem.at[n])
        for n, (src, dst) in enumerate(
            ((fc1_in, fc1), (fc2_in, fc2), (tok_in, tok), (wq_in, wq), (og_in, og), (wp_in, wp))
        )
    ]
    for copy in loads:
        copy.start()
    barrier = pltpu.get_barrier_semaphore()
    peers = [class_peer(d) for d in range(1, 8)]
    peers += [plane_peer(d) for d in range(1, 16)]
    for peer in peers:
        pl.semaphore_signal(barrier, inc=1, device_id=peer, device_id_type=MESH)

    def remote(src, dst, send, recv, peer):
        return pltpu.make_async_remote_copy(
            src_ref=src, dst_ref=dst, send_sem=send, recv_sem=recv, device_id=peer, device_id_type=MESH
        )

    def param(part):
        return small[D * part : D * part + D].reshape(1, D)

    pending = []

    def start(copy):
        copy.start()
        pending.append(copy)
        return copy

    def shard(place):
        half = pl.ds(pl.multiple_of(core * (D // 2), 16), D // 2)
        half_at = pl.ds(pl.multiple_of(place * D + core * (D // 2), 16), D // 2)
        return w1.at[half, D * place : D * place + D], w2.at[half_at, :]

    def near(d, n):
        return remote(shard(0)[n], shard(PLACE[4 - d])[n], w_send.at[d // 2, n], w_recv.at[d // 2, n], along_x(d))

    def far(n):
        d = 3 - 2 * n
        return remote(shard(1 + n)[n], shard(3)[n], w_send.at[2, n], w_recv.at[2, n], along_x(d))

    def bias_copy(d):
        return remote(b1.at[0], b1.at[PLACE[4 - d]], b_send.at[d - 1], b_recv.at[d - 1], along_x(d))

    def across(place, n):
        came = shard(place)[n]
        return remote(came, came, pair_send.at[place - 1, n], pair_recv.at[place - 1, n], (pair, mlp))

    for copy in loads[:2]:
        copy.wait()
    w1[:, :D] = fc1[...].astype(BF16)
    w2[:D, :] = fc2[...].astype(BF16)
    b1[0, 0:4] = jnp.broadcast_to(fc1_b[...].reshape(1, D), (4, D))
    b1[0, 4:8] = jnp.broadcast_to(fc1_state[...].reshape(1, D), (4, D))
    pl.semaphore_wait(barrier, 22)
    for n in range(2):
        for d in (1, 3):
            start(near(d, n))
    for d in range(1, 4):
        start(bias_copy(d))

    live = live_windows[0]
    for n in range(1, GROUPS * PER):
        live = live + live_windows[n]
    live = live * SPAN
    prologue(region, table, emask, bias, mask)
    for copy in loads[2:]:
        copy.wait()
    widen(tok, x_ref)
    for g in range(SETS):
        for part in range(3):
            wq_b[:, D * g + 128 * part : D * g + 128 * part + 128] = wq[
                :, D * part + 128 * g : D * part + 128 * g + 128
            ].astype(BF16)
    wp_b[...] = wp[...].astype(BF16)
    sums[...] = jnp.zeros_like(sums)
    b1_acc[...] = jnp.zeros_like(b1_acc)
    tacc[...] = jnp.zeros_like(tacc)
    att = dqkv.at[:, :D]
    xh2 = dqkv.at[:, D : 2 * D]
    dqkv_b = ig.at[:, :QKV]
    dqkv[:, :D] = jnp.zeros((ROWS, D), F32)

    for a in range(GROUPS):
        for r in range(0, G_TOK, 56):
            src = a * G_TOK + r
            low = src // 16 * 16
            rows = og[low : low + 64 if low + 64 <= TOK else TOK, :].astype(F32)[src - low : src - low + 56]
            keep = iota((56, D), 0) + src < live
            x = jnp.where(keep, rows, 0.0)
            s2[r : r + 56, :] = x
            sums[7] += fold_rows(x)
        s2[G_TOK:G_ROWS, :] = jnp.zeros((G_ROWS - G_TOK, D), F32)
        back[a * G_ROWS : (a + 1) * G_ROWS, :] = s2[...].astype(BF16)

    shift_q = jnp.concatenate(
        [
            part[:, 128 * g : 128 * g + 128]
            for g in range(SETS)
            for part in (param(2), jnp.zeros((1, D), F32), param(3))
        ],
        axis=1,
    )

    @pl.loop(0, 5, unroll=5)
    def _(t):
        for c in range(15):
            rows = pl.ds(pl.multiple_of(t * 240 + c * 16, 16), 16)
            scaled, inverse = normalize(x_ref[rows, :])
            xh1[rows, :] = scaled
            inv1[rows, :] = inverse
            n1[rows, :] = (scaled * param(0) + param(1)).astype(BF16)

    @pl.loop(0, 5, unroll=5)
    def _(t):
        rows = pl.ds(pl.multiple_of(t * 240, 16), 240)
        qkv[rows, :] = (dot(n1[rows, :], wq_b[...]) + shift_q).astype(BF16)

    def scores_of(a, b, g):
        rows = pl.ds(pl.multiple_of(a * G_ROWS + b * 48, 16), CHUNK)
        q = qkv[rows, D * g : D * g + 128]
        k = qkv[rows, D * g + 128 : D * g + 256]
        return dot_nt(k, spread(q, emask[b]))

    def attend(a, b, g, raw):
        rows = pl.ds(pl.multiple_of(a * G_ROWS + b * 48, 16), CHUNK)
        v = qkv[rows, D * g + 256 : D * g + 384]
        scores = raw[:KEYS] * SCALE + (bias[b, g] + mask[a * PER + b])
        p = jnp.exp(scores - jnp.max(scores, axis=0, keepdims=True))
        p = p * (1.0 / jnp.sum(p, axis=0, keepdims=True))
        probs[a * PER + b, g] = p
        return dot_tn(pad_keys(p).astype(BF16), v)

    def attended(a, b, g, full):
        rows = pl.ds(pl.multiple_of(a * G_ROWS + b * 48, 16), CHUNK)
        i = iota((CHUNK, 128), 0)
        att[rows, 128 * g : 128 * g + 128] += jnp.where((i >= b) & (i < b + SPAN), collect(full), 0.0)

    @pl.loop(0, 4)
    def _(pair_at):
        blocks = [[(a, 2 * pair_at + b, g) for a in range(GROUPS)] for b in range(2) for g in range(SETS)]
        ahead = [scores_of(*unit) for unit in blocks[0]]
        for n, units in enumerate(blocks):
            raws = ahead
            if n + 1 < len(blocks):
                ahead = [scores_of(*unit) for unit in blocks[n + 1]]
            fulls = [attend(*unit, raw) for unit, raw in zip(units, raws)]
            for unit, full in zip(units, fulls):
                attended(*unit, full)

    for n in range(2):
        for d in (1, 3):
            near(d, n).wait_recv()
        start(far(n))
    for place in (1, 2):
        for n in range(2):
            start(across(place, n))
    for d in range(1, 4):
        bias_copy(d).wait_recv()

    @pl.loop(0, GROUPS, unroll=3)
    def _(a):
        rows = pl.ds(pl.multiple_of(a * G_ROWS, 16), G_ROWS)
        att_b[rows, :] = att[rows, :].astype(BF16)
        s1[...] = dot(att_b[rows, :], wp_b[...])

        for c in range(25):
            here = pl.ds(pl.multiple_of(a * G_ROWS + 16 * c, 16), 16)
            middle = x_ref[here, :] + (s1[16 * c : 16 * c + 16, :] + param(4))
            stage[here, :] = middle
            scaled, inverse = normalize(middle)
            xh2[here, :] = scaled
            inv2[here, :] = inverse
            n2[here, :] = (scaled * param(5) + param(6)).astype(BF16)

    for nt in range(6):
        if nt in (1, 3):
            for n in range(2):
                across(1 + nt // 2, n).wait_recv()
        if nt == 3:
            for n in range(2):
                far(n).wait_recv()
                start(across(3, n))
        if nt == 4:
            for n in range(2):
                across(3, n).wait_recv()
        cols = slice(256 * nt, 256 * nt + 256)
        shift = jnp.concatenate(
            [b1[c // 3, 0:1, 128 * (c % 3) : 128 * (c % 3) + 128] for c in (2 * nt, 2 * nt + 1)], axis=1
        )

        @pl.loop(0, 5)
        def _(mt):
            rows = pl.ds(pl.multiple_of(mt * 240, 16), 240)
            inner = dot(n2[rows, :], w1[:, cols]) + shift
            up = dot_nt(back[rows, :], w2[cols, :])
            total = b1_acc[:, cols]
            for c in range(15):
                act, slope = gelu_parts(inner[16 * c : 16 * c + 16])
                here = pl.ds(pl.multiple_of(mt * 240 + 16 * c, 16), 16)
                hidden[here, cols] = act.astype(BF16)
                grad = (up[16 * c : 16 * c + 16] * slope).astype(BF16)
                ig[here, cols] = grad
                total = total + fold_rows(grad.astype(F32))
            b1_acc[:, cols] = total

    g2 = dot_tn(hidden[...], back[...]).astype(BF16)
    g1 = dot_tn(n2[...], ig[...]).astype(BF16)
    for m in range(4):
        fcl[0, m] = g1[:, D * m : D * m + D].reshape(4, 96, D)
        fcl[1, m] = g2[D * m : D * m + D].reshape(4, 96, D)
    fc_one = [start(remote(fcl.at[1 - core, m], fr1.at[m], f1s.at[m], f1r.at[m], (pair, mlp))) for m in range(4)]

    def middle_back(a):
        rows = slice(a * G_ROWS, (a + 1) * G_ROWS)
        held = (s1, s2)[a % 2]
        held[...] = dot_nt(ig[rows, :], w1[...])
        for c in range(25):
            here = slice(16 * c, 16 * c + 16)
            at = slice(a * G_ROWS + 16 * c, a * G_ROWS + 16 * c + 16)
            u = held[here, :]
            scaled = xh2[at, :]
            sums[5] += fold_rows(u * scaled)
            sums[6] += fold_rows(u)
            mg = normalize_back(u, param(5), scaled, inv2[at, :]) + back[at, :].astype(F32)
            x_ref[at, :] = mg
            low = mg.astype(BF16)
            n2[at, :] = low
            sums[4] += fold_rows(low.astype(F32))

    def out_copy(a):
        return pltpu.make_async_copy(
            stage.at[pl.ds(a * G_ROWS, G_TOK)], out_to.at[pl.ds(a * G_TOK, G_TOK)], out_sem.at[a]
        )

    def block_out(a):
        rows = slice(a * G_ROWS, (a + 1) * G_ROWS)
        held = (s1, s2)[a % 2]
        held[...] = dot(hidden[rows, :], w2[...])
        for c in range(25):
            at = slice(a * G_ROWS + 16 * c, a * G_ROWS + 16 * c + 16)
            r = stage[at, :] + (held[16 * c : 16 * c + 16, :] + param(7))
            keep = iota((16, D), 0) + (a * G_TOK + 16 * c) < live
            stage[at, :] = jnp.where(keep, r, 0.0)
        out_copy(a).start()

    p = iota((D, D), 0)
    inner_p = p % 48
    owned = 24 * (inner_p // 3) + 12 * (p // 192) + 3 * ((p // 48) % 4) + inner_p % 3
    order = jnp.where(iota((D, D), 1) == owned, 1.0, 0.0).astype(BF16)

    def ordered(grad):
        return dot(order, grad.astype(BF16)).astype(BF16).reshape(2, 4, 48, D)

    def at_one(n):
        return remote(atl.at[n, 1 - core], ar1.at[n], a1s.at[n], a1r.at[n], (pair, mlp))

    def at_add_one(n):
        at_one(n).wait_recv()
        for i in range(4):
            ar1[n, i] = (ar1[n, i].astype(F32) + atl[n, core, i].astype(F32)).astype(BF16)
        for d in range(1, 4):
            start(remote(ar1.at[n, (mlp + d) % 4], ar2.at[n, d - 1], a2s.at[n, d - 1], a2r.at[n, d - 1], along_x(d)))

    def near_axis(d):
        return ((z + d * core) % 4) * 8 + ((y + d * (1 - core)) % 4) * 2 + core, mlp

    def other_axis(d):
        return ((z + d * (1 - core)) % 4) * 8 + ((y + d * core) % 4) * 2 + core, mlp

    near_at, other_at = y * (1 - core) + z * core, z * (1 - core) + y * core

    def at_add_two(n):
        total = ar1[n, mlp].astype(F32)
        for d in range(1, 4):
            remote(ar1.at[n, 0], ar2.at[n, d - 1], a2s.at[n, d - 1], a2r.at[n, d - 1], along_x(d)).wait_recv()
            total = total + ar2[n, d - 1].astype(F32)
        ar3[n, near_at] = total.astype(BF16)
        for d in range(1, 4):
            start(remote(ar3.at[n, near_at], ar3.at[n, near_at], a3s.at[n, d - 1], a3r.at[n, d - 1], near_axis(d)))

    def at_add_three(n):
        for d in range(1, 4):
            came = ar3.at[n, (near_at + 4 - d) % 4]
            remote(came, came, a3s.at[n, d - 1], a3r.at[n, d - 1], near_axis(d)).wait_recv()
        total = ar3[n, 0].astype(F32) + ar3[n, 1].astype(F32)
        ar4[n, other_at] = (total + ar3[n, 2].astype(F32) + ar3[n, 3].astype(F32)).astype(BF16)
        for d in range(1, 4):
            start(remote(ar4.at[n, other_at], ar4.at[n, other_at], a4s.at[n, d - 1], a4r.at[n, d - 1], other_axis(d)))

    def at_finish(n):
        for d in range(1, 4):
            came = ar4.at[n, (other_at + 4 - d) % 4]
            remote(came, came, a4s.at[n, d - 1], a4r.at[n, d - 1], other_axis(d)).wait_recv()
        total = ar4[n, 0].astype(F32) + ar4[n, 1].astype(F32)
        at_total[n] = total + ar4[n, 2].astype(F32) + ar4[n, 3].astype(F32)

    def to_axes(dx, dy, dz):
        return ((z + dz) % 4) * 8 + ((y + dy) % 4) * 2 + core, (mlp + dx) % 4

    def first_axis(d):
        return to_axes(d * (1 - core), 0, d * core)

    def second_axis(d):
        return to_axes(d * core, d * (1 - core), 0)

    def third_axis(d):
        return to_axes(0, d * core, d * (1 - core))

    def last_axis(d):
        return to_axes(0, d * (1 - core), d * core)

    block_at = y * (1 - core) + z * core
    second = y * (1 - core)
    third = z * (1 - core) + y * core

    def fc_two(d):
        return remote(fr1.at[0], fr2.at[d - 1], f2s.at[d - 1], f2r.at[d - 1], first_axis(d))

    def fc_add_one():
        for m in range(4):
            fc_one[m].wait_recv()
            for i in range(4):
                fr1[m, i] = (fr1[m, i].astype(F32) + fcl[core, m, i].astype(F32)).astype(BF16)

        @pl.when(core == 0)
        def _():
            for d in range(1, 4):
                remote(fr1.at[PLACE[d]], fr2.at[d - 1], f2s.at[d - 1], f2r.at[d - 1], first_axis(d)).start()

        @pl.when(core == 1)
        def _():
            for d in range(1, 4):
                remote(fr1.at[:, (z + d) % 4], fr2.at[d - 1], f2s.at[d - 1], f2r.at[d - 1], first_axis(d)).start()

    def fc_add_two():
        for d in range(1, 4):
            fc_two(d).wait_recv()
        for i in range(4):
            total = fr1[i * core, i * (1 - core) + z * core].astype(F32)
            for d in range(1, 4):
                total = total + fr2[d - 1, i].astype(F32)
            ft[i] = total.astype(BF16)
        for d in range(1, 4):
            to = (1 - core) * ((y + d) % 4) + core * PLACE[d]
            start(remote(ft.at[to], fr3.at[d - 1], f3s.at[d - 1], f3r.at[d - 1], second_axis(d)))

    def fc_add_three():
        total = ft[second].astype(F32)
        for d in range(1, 4):
            remote(ft.at[0], fr3.at[d - 1], f3s.at[d - 1], f3r.at[d - 1], second_axis(d)).wait_recv()
            total = total + fr3[d - 1].astype(F32)
        fr4[third] = total.astype(BF16)
        for d in range(1, 4):
            start(remote(fr4.at[third], fr4.at[third], f4s.at[d - 1], f4r.at[d - 1], third_axis(d)))

    def fc_add_four():
        for d in range(1, 4):
            came = fr4.at[(third + 4 - d) % 4]
            remote(came, came, f4s.at[d - 1], f4r.at[d - 1], third_axis(d)).wait_recv()
        total = fr4[0].astype(F32) + fr4[1].astype(F32)
        fin_b[core, block_at] = (total + fr4[2].astype(F32) + fr4[3].astype(F32)).astype(BF16)
        for d in range(1, 4):
            place = fin_b.at[core, block_at]
            start(remote(place, place, f5s.at[d - 1], f5r.at[d - 1], last_axis(d)))

    def fc_spread():
        for d in range(1, 4):
            place = fin_b.at[core, (block_at + 4 - d) % 4]
            remote(place, place, f5s.at[d - 1], f5r.at[d - 1], last_axis(d)).wait_recv()
        start(remote(fin_b.at[core], fin_b.at[core], f7s.at[0], f7r.at[0], (pair, mlp)))

    mine_at, plane_at = 4 * core + mlp, 4 * z + y

    def vec_one(n):
        for d in range(1, 8):
            place = vx.at[n, mine_at]
            start(remote(place, place, vxs.at[n, d - 1], vxr.at[n, d - 1], class_peer(d)))

    def vec_two(n):
        for d in range(1, 8):
            place = vx.at[n, (mlp + 8 - d) % 4 + 4 * (core if d < 4 else 1 - core)]
            remote(place, place, vxs.at[n, d - 1], vxr.at[n, d - 1], class_peer(d)).wait_recv()
        total = vx[n, 0]
        for i in range(1, 8):
            total = total + vx[n, i]
        vy[n, plane_at] = total
        for d in range(1, 16):
            place = vy.at[n, plane_at]
            start(remote(place, place, vys.at[n, d - 1], vyr.at[n, d - 1], plane_peer(d)))

    def vec_three(n):
        for d in range(1, 16):
            place = vy.at[n, 4 * ((z + 4 - d // 4) % 4) + (y + 4 - d % 4) % 4]
            remote(place, place, vys.at[n, d - 1], vyr.at[n, d - 1], plane_peer(d)).wait_recv()
        total = vy[n, 0]
        for i in range(1, 16):
            total = total + vy[n, i]
        vec[8 * n : 8 * n + 8, :] = total

    middle_back(0)
    middle_back(1)
    fc_add_one()
    middle_back(2)

    atl[3] = ordered(dot_tn(att_b[...], n2[...]))
    start(at_one(3))

    @pl.loop(0, GROUPS, unroll=3)
    def _(a):
        rows = pl.ds(pl.multiple_of(a * G_ROWS, 16), G_ROWS)
        att_b[rows, :] = dot_nt(n2[rows, :], wp_b[...]).astype(BF16)

    dqkv[...] = jnp.zeros_like(dqkv)

    def attention_back(g, half):
        def first(a, b):
            rows = pl.ds(a * G_ROWS + b * 48, CHUNK)
            v = qkv[rows, D * g + 256 : D * g + 384]
            da = spread(att_b[rows, 128 * g : 128 * g + 128], emask[b])
            return da, dot_nt(v, da)

        def inner_grad(a, b, dp):
            p = probs[a * PER + b, g]
            pd = p * dp[:KEYS]
            return pad_keys(p).astype(BF16), pad_keys(pd - p * jnp.sum(pd, axis=0, keepdims=True)).astype(BF16)

        def last(a, b, da, p, ds):
            rows = pl.ds(a * G_ROWS + b * 48, CHUNK)
            q = qkv[rows, D * g : D * g + 128]
            k = qkv[rows, D * g + 128 : D * g + 256]
            dv = dot(p, da)
            dk = dot(ds, spread(q, emask[b])) * SCALE
            dq = collect(dot_tn(ds, k)) * SCALE
            dqkv[rows, 384 * g : 384 * g + 128] += dq
            dqkv[rows, 384 * g + 128 : 384 * g + 256] += dk
            dqkv[rows, 384 * g + 256 : 384 * g + 384] += dv

        bs = range(4 * half, 4 * half + 4)
        ahead = [first(a, bs[0]) for a in range(GROUPS)]
        for b in bs:
            held = ahead
            if b + 1 in bs:
                ahead = [first(a, b + 1) for a in range(GROUPS)]
            grads = [inner_grad(a, b, held[a][1]) for a in range(GROUPS)]
            tacc[b, g] = sum(ds.astype(F32)[:KEYS] for _, ds in grads)
            for a in range(GROUPS):
                last(a, b, held[a][0], *grads[a])

    def qkv_grad(g):
        group = slice(384 * g, 384 * g + 384)

        @pl.loop(0, 5, unroll=5)
        def _(t):
            for c in range(15):
                rows = pl.ds(pl.multiple_of(t * 240 + c * 16, 16), 16)
                low = dqkv[rows, group].astype(BF16)
                dqkv_b[rows, group] = low
                wide = low.astype(F32)
                sums[2, :, 128 * g : 128 * g + 128] += fold_rows(wide[:, :128])
                sums[3, :, 128 * g : 128 * g + 128] += fold_rows(wide[:, 256:])

        atl[g] = ordered(dot_tn(n1[...], dqkv_b[:, group]))
        start(at_one(g))

    for part in range(4):
        vx[0, mine_at, part : part + 1, :] = jnp.sum(sums[4 + part], axis=0, keepdims=True)
    for m in range(4):
        d = (m + 4 - mlp) % 4
        place = d + d // 2 - 2 * (d // 3)
        cols = pl.ds(pl.multiple_of(place * D, 128), D)
        vx[0, mine_at, 4 + m : 5 + m, :] = jnp.sum(b1_acc[:, cols], axis=0, keepdims=True)
    vec_one(0)

    def table_back(g, n):
        j = iota((KEYS, 256), 0)
        amount = jnp.maximum(84 - embed(j), 0)
        total = tacc[0, g]
        for b in range(1, PER):
            total = total + pltpu.roll(pltpu.roll(tacc[b, g], KEYS - b, 0), LANES - b, 1)
        for h in range(4):
            lane_from = iota((LANES, 256), 0) - CHUNK * h
            pick = (iota((LANES, 256), 1) == embed(lane_from)) & (lane_from >= 0) & (lane_from < SPAN)
            wide = barrel(dot_exact(total, jnp.where(pick, 1.0, 0.0)), amount, True)
            wide = jnp.where(j < SPAN, wide, 0.0)
            vx[n, mine_at, 4 * (g % 2) + h : 4 * (g % 2) + h + 1, :] = jnp.concatenate(
                [jnp.sum(wide, axis=0, keepdims=True), jnp.zeros((1, 128), F32)], axis=1
            )

    attention_back(0, 0)
    attention_back(0, 1)
    qkv_grad(0)
    attention_back(1, 0)
    attention_back(1, 1)
    fc_add_two()
    qkv_grad(1)
    at_add_one(3)
    at_add_one(0)
    vec_two(0)
    attention_back(2, 0)
    at_add_one(1)
    attention_back(2, 1)
    qkv_grad(2)
    fc_add_three()
    at_add_one(2)

    def gin_copy(a):
        src = pl.ds(pl.multiple_of(a * G_ROWS, 8), G_TOK)
        dst = pl.ds(pl.multiple_of(a * G_TOK, 8), G_TOK)
        return pltpu.make_async_copy(x_ref.at[src], gin_to.at[dst], out_sem.at[3 + a])

    @pl.loop(0, GROUPS)
    def _(a):
        rows = pl.ds(pl.multiple_of(a * G_ROWS, 16), G_ROWS)
        s2[...] = dot_nt(dqkv_b[rows, :], wq_b[...])
        for c in range(25):
            here = slice(16 * c, 16 * c + 16)
            at = pl.ds(pl.multiple_of(a * G_ROWS + 16 * c, 16), 16)
            u = s2[here, :]
            scaled = xh1[at, :]
            sums[0] += fold_rows(u * scaled)
            sums[1] += fold_rows(u)
            x_ref[at, :] = normalize_back(u, param(0), scaled, inv1[at, :]) + x_ref[at, :]
        gin_copy(a).start()

    at_add_two(3)
    at_add_two(0)
    table_back(0, 1)
    table_back(1, 1)
    vec_one(1)
    at_add_two(1)
    table_back(2, 2)
    for part in range(4):
        vx[2, mine_at, 4 + part : 5 + part, :] = jnp.sum(sums[part], axis=0, keepdims=True)
    vec_one(2)
    vec_three(0)
    fc_add_four()
    at_add_two(2)
    block_out(0)
    block_out(1)
    at_add_three(3)
    at_add_three(0)
    block_out(2)
    at_add_three(1)
    vec_two(1)
    vec_two(2)
    at_add_three(2)
    fc_spread()
    at_finish(3)
    at_finish(0)
    at_finish(1)

    remote(fin_b.at[1 - core], fin_b.at[1 - core], f7s.at[0], f7r.at[0], (pair, mlp)).wait_recv()
    for half in range(2):
        for n in range(4):
            fin[half, n] = fin_b[half, n].astype(F32)
    fin_copy = pltpu.make_async_copy(fin, fin_to, out_sem.at[6])
    fin_copy.start()
    eye = iota((D, D), 0) == iota((D, D), 1)

    def to_row(column):
        return jnp.sum(jnp.where(eye, column, 0.0), axis=0, keepdims=True)

    up = fin[0].reshape(D, D)
    down = fin[1].reshape(D, D)
    up_squares = up * up
    down_squares = down * down
    up_col = DECAY * fc1_col[...].reshape(1, D) + (1.0 - DECAY) * (
        jnp.sum(up_squares, axis=0, keepdims=True) * (1.0 / D) + EPS_SQ
    )
    down_row = DECAY * to_column(fc2_row[...].reshape(1, D), eye) + (1.0 - DECAY) * (row_mean(down_squares) + EPS_SQ)
    fst[mlp, 0:1] = to_row(jnp.sum(up_squares, axis=1, keepdims=True))
    fst[mlp, 1:2] = to_row(jnp.sum(up_squares * (1.0 / up_col), axis=1, keepdims=True))
    fst[mlp, 2:3] = jnp.sum(down_squares, axis=0, keepdims=True)
    fst[mlp, 3:4] = jnp.sum(down_squares * (1.0 / down_row), axis=0, keepdims=True)
    fst[mlp, 4:5] = jnp.broadcast_to(jnp.sum(down_row, axis=0, keepdims=True), (1, D))
    fst[mlp, 5:6] = up_col
    fst[mlp, 6:7] = to_row(down_row)
    fst[mlp, 7:8] = jnp.zeros((1, D), F32)
    for d in range(1, 4):
        start(remote(fst.at[mlp], fst.at[mlp], f8s.at[d - 1], f8r.at[d - 1], along_x(d)))

    vec_three(1)

    offset = 48 - 3 * plane_at
    block_rows = pl.ds(pl.multiple_of(24 * (win // 2), 8), 24)
    shift = 24 - 3 * mine_at
    rolled = pltpu.roll(wq[block_rows, :], shift, 0)[:8]
    for part in range(3):
        own_wq[8 * part : 8 * part + 8, :] = rolled[:, D * part : D * part + D]
    own_wp[...] = pltpu.roll(wp[block_rows, :], shift, 0)[:8]

    r48 = iota((48, D), 0)
    pick = iota((48, D), 1) == 24 * (r48 // 3) + 12 * core + 3 * mlp + r48 % 3

    def rows_new(state, mean):
        old = jnp.sum(jnp.where(pick, state, 0.0), axis=1, keepdims=True)
        return DECAY * old + (1.0 - DECAY) * (mean + EPS_SQ)

    at_finish(2)
    squares = [at_total[n] * at_total[n] for n in range(4)]
    qkv_new_row = rows_new(
        qkv_row[...].reshape(1, D), row_mean(squares[0] + squares[1] + squares[2]) * (1.0 / 3.0)
    )
    proj_new_row = rows_new(proj_row[...].reshape(1, D), row_mean(squares[3]))
    for n in range(4):
        over = squares[n] * (1.0 / (qkv_new_row if n < 3 else proj_new_row))
        ast[mine_at, n : n + 1] = jnp.sum(squares[n], axis=0, keepdims=True)
        ast[mine_at, 4 + n : 5 + n] = jnp.sum(over, axis=0, keepdims=True)
    ast[mine_at, 8:9] = jnp.broadcast_to(jnp.sum(qkv_new_row, axis=0, keepdims=True), (1, D))
    ast[mine_at, 9:10] = jnp.broadcast_to(jnp.sum(proj_new_row, axis=0, keepdims=True), (1, D))
    ast[mine_at, 10:16] = jnp.zeros((6, D), F32)

    def at_five(d):
        place = ast.at[mine_at]
        return remote(place, place, a5s.at[d - 1], a5r.at[d - 1], class_peer(d))

    for d in range(1, 8):
        start(at_five(d))

    for n in range(4):
        own_g[8 * n : 8 * n + 8, :] = pltpu.roll(at_total[n], offset, 0)[:8]
        b1_all[8 * n : 8 * n + 8, :] = b1[n]
    own_r[0:8, :] = pltpu.roll(jnp.broadcast_to(qkv_new_row, (48, D)), offset, 0)[:8]
    own_r[8:16, :] = pltpu.roll(jnp.broadcast_to(proj_new_row, (48, D)), offset, 0)[:8]

    for d in range(1, 4):
        place = fst.at[(mlp + 4 - d) % 4]
        remote(place, place, f8s.at[d - 1], f8r.at[d - 1], along_x(d)).wait_recv()
    fc_sums[0:8, :] = (fst[0] + fst[1]) + (fst[2] + fst[3])
    fc_sums[8:16, :] = fst[mlp]
    vec_three(2)

    for d in range(1, 8):
        place = ast.at[(mlp + 8 - d) % 4 + 4 * (core if d < 4 else 1 - core)]
        remote(place, place, a5s.at[d - 1], a5r.at[d - 1], class_peer(d)).wait_recv()
    total = ast[0]
    for n in range(1, 8):
        total = total + ast[n]
    at_sums[...] = total

    for a in range(GROUPS):
        gin_copy(a).wait()
        out_copy(a).wait()
    fin_copy.wait()
    for copy in pending:
        copy.wait_send()
    for d in range(1, 4):
        fc_two(d).wait_send()


def to_column(row, eye):
    return jnp.sum(jnp.where(eye, row, 0.0), axis=1, keepdims=True)


def block(live_windows, region, tok, og, wq, wp, fc1, fc2, *arrays):
    sd = jax.ShapeDtypeStruct
    vm = pltpu.VMEM
    dma = pltpu.SemaphoreType.DMA
    return pl.pallas_call(
        block_kernel,
        out_shape=[
            sd((TOK, D), F32),
            sd((TOK, D), F32),
            sd((2, 4, 96, D), F32),
            sd((168, D), F32),
        ],
        in_specs=[pl.BlockSpec(memory_space=pltpu.SMEM), pl.BlockSpec(memory_space=vm)]
        + [pl.BlockSpec(memory_space=pl.ANY)] * 6
        + [pl.BlockSpec(memory_space=vm)] * len(arrays),
        out_specs=[pl.BlockSpec(memory_space=pl.ANY)] * 3 + [pl.BlockSpec(memory_space=vm)],
        scratch_shapes=[
            vm((ROWS, D), F32),
            vm((ROWS, D), F32),
            vm((ROWS, 1), F32),
            vm((ROWS, 1), F32),
            vm((ROWS, D), BF16),
            vm((ROWS, D), BF16),
            vm((ROWS, QKV), BF16),
            vm((ROWS, D), BF16),
            vm((GROUPS * PER, SETS, KEYS, LANES), F32),
            vm((ROWS, D), BF16),
            vm((ROWS, FF), BF16),
            vm((ROWS, FF), BF16),
            vm((ROWS, QKV), F32),
            vm((PER, LANES, 128), BF16),
            vm((PER, SETS, KEYS, LANES), F32),
            vm((GROUPS * PER, KEYS, LANES), F32),
            vm((PER, SETS, KEYS, LANES), F32),
            vm((G_ROWS, D), F32),
            vm((G_ROWS, D), F32),
            vm((8, 8, D), F32),
            vm((8, FF), F32),
            vm((D, QKV), BF16),
            vm((D, D), BF16),
            vm((D, FF), BF16),
            vm((FF, D), BF16),
            vm((TOK, D), BF16),
            vm((TOK, D), BF16),
            vm((D, QKV), F32),
            vm((D, D), F32),
            vm((D, D), F32),
            vm((D, D), F32),
            vm((2, 4, 96, D), F32),
            vm((2, 4, 96, D), BF16),
            vm((4, 8, D), F32),
            vm((ROWS, D), F32),
            dma((6,)), dma((7,)),
            vm((2, 4, 4, 96, D), BF16),
            vm((4, 4, 96, D), BF16),
            vm((3, 4, 96, D), BF16),
            vm((4, 96, D), BF16),
            vm((3, 96, D), BF16),
            vm((4, 96, D), BF16),
            vm((4, 8, D), F32),
            vm((4, 2, 4, 48, D), BF16),
            vm((4, 4, 48, D), BF16),
            vm((4, 3, 48, D), BF16),
            vm((4, 4, 48, D), BF16),
            vm((4, 4, 48, D), BF16),
            vm((8, 16, D), F32),
            vm((3, 8, 8, D), F32),
            vm((3, 16, 8, D), F32),
            vm((4, 48, D), F32),
            dma((3, 2)), dma((3, 2)), dma((3,)), dma((3,)), dma((3, 2)), dma((3, 2)),
            dma((4,)), dma((4,)),
            dma((3,)), dma((3,)), dma((3,)), dma((3,)), dma((3,)), dma((3,)),
            dma((3,)), dma((3,)), dma((1,)), dma((1,)), dma((3,)), dma((3,)),
            dma((4,)), dma((4,)),
            dma((4, 3)), dma((4, 3)), dma((4, 3)), dma((4, 3)), dma((4, 3)), dma((4, 3)),
            dma((7,)), dma((7,)),
            dma((3, 7)), dma((3, 7)), dma((3, 15)), dma((3, 15)),
        ],
        compiler_params=pltpu.CompilerParams(
            vmem_limit_bytes=63 * 1024 * 1024, collective_id=0, has_side_effects=True
        ),
        cost_estimate=pl.CostEstimate(flops=14_000_000_000, bytes_accessed=20_000_000, transcendentals=3_000_000),
        name="block",
    )(live_windows, region, tok, og, wq, wp, fc1, fc2, *arrays)


def finish_kernel(
    fin, fc1, fc2, out_from, gin_from, pack, fc1_b, fc1_row, fc2_col, qkv_col, proj_col,
    small, small_state, table, table_state,
    qkv_grad, qkv_row_new, qkv_col_new, qkv_new, qkv_low, proj_grad, proj_row_new, proj_col_new, proj_new, proj_low,
    fc1_grad, fc1_row_new, fc1_col_new, fc1_new, fc1_low, fc2_grad, fc2_row_new, fc2_col_new, fc2_new, fc2_low,
    b1_grad, b1_state_new, b1_new, small_grad, small_state_new, small_new, table_grad, table_state_new, table_new,
    out_to, gin_to, held, sem_in, sem_out,
):
    vec, fc_sums, at_sums, own_g, own_wq, own_wp, b1, own_r = packed(pack)
    def parts(src, dst, n):
        for i in range(4):
            rows = pl.ds(304 * i, 304 if i < 3 else TOK - 912)
            here = held.at[n, rows]
            yield (
                pltpu.make_async_copy(src.at[rows], here, sem_in.at[n, i]),
                pltpu.make_async_copy(here, dst.at[rows], sem_out.at[n, i]),
            )

    copies = list(parts(out_from, out_to, 0)) + list(parts(gin_from, gin_to, 1))
    for copy, _ in copies:
        copy.start()
    mlp = lax.axis_index("mlp")
    eye = iota((D, D), 0) == iota((D, D), 1)
    eye8 = iota((8, 128), 0) == iota((8, 128), 1)

    def line(x):
        return x.reshape(1, -1)

    def total(x):
        return jnp.sum(jnp.sum(x, axis=0, keepdims=True), axis=1, keepdims=True)

    def fresh(old, mean):
        return DECAY * old + (1.0 - DECAY) * (mean + EPS_SQ)

    def owned(grads, cols, over, row, row_total, weight, col_old, rate, outs):
        grad_out, row_out, col_out, new_out, low_out = outs
        width = grads.shape[1]
        col_new = fresh(line(col_old[...]), cols * (1.0 / D))
        mean = row_total * (1.0 / D)
        norm = mean * jnp.sum(over * (1.0 / col_new), axis=1, keepdims=True) * (1.0 / (D * width))
        step = grads * lax.rsqrt(row * col_new * (1.0 / mean))
        new = weight - rate * (step * clip_scale(norm))
        grad_out[...] = grads[:3]
        row_out[...] = jnp.sum(jnp.where(eye8, row, 0.0), axis=0)[:3]
        col_out[...] = col_new.reshape(width)
        new_out[...] = new[:3]
        low_out[...] = new.astype(BF16)[:3]

    def by_part(take):
        return jnp.concatenate([take(g)[:, 128 * p : 128 * p + 128] for p in range(3) for g in range(SETS)], axis=1)

    owned(
        by_part(lambda g: own_g[8 * g : 8 * g + 8, :]), by_part(lambda g: at_sums[g : g + 1, :]),
        by_part(lambda g: at_sums[4 + g : 5 + g, :]), own_r[0:8, :1], at_sums[8:9, :1],
        jnp.concatenate([own_wq[8 * part : 8 * part + 8, :] for part in range(3)], axis=1), qkv_col,
        D ** (-0.5), (qkv_grad, qkv_row_new, qkv_col_new, qkv_new, qkv_low),
    )
    owned(
        own_g[24:32, :], at_sums[3:4, :], at_sums[7:8, :], own_r[8:16, :1], at_sums[9:10, :1], own_wp[...], proj_col,
        (D // 8) ** (-0.5), (proj_grad, proj_row_new, proj_col_new, proj_new, proj_low),
    )

    for copy, then in copies:
        copy.wait()
        then.start()

    def update(grad, weight, row, col, mean, norm, rate, grad_out, new_out, low_out):
        row = row * (1.0 / mean)
        factor = rate * clip_scale(norm)
        for r in range(0, D, 48):
            rows = slice(r, r + 48)
            g = grad[rows, :]
            new = weight[rows, :] - (g * lax.rsqrt(row[rows] * col)) * factor
            grad_out[rows, :] = g
            new_out[rows, :] = new
            low_out[rows, :] = new.astype(BF16)

    row_new = fresh(line(fc1_row[...]), fc_sums[0:1, :] * (1.0 / FF))
    mean = row_mean(row_new)
    norm = mean * row_mean(fc_sums[1:2, :] * (1.0 / row_new)) * (1.0 / FF)
    fc1_row_new[...] = row_new.reshape(D)
    fc1_col_new[...] = fc_sums[13]
    update(
        fin.at[0], fc1, to_column(row_new, eye), fc_sums[13:14, :], mean, norm, D ** (-0.5),
        fc1_grad, fc1_new, fc1_low,
    )
    col_new = fresh(line(fc2_col[...]), fc_sums[2:3, :] * (1.0 / FF))
    mean = fc_sums[4:5, :1] * (1.0 / FF)
    norm = mean * row_mean(fc_sums[3:4, :] * (1.0 / col_new)) * (1.0 / FF)
    fc2_row_new[...] = fc_sums[14]
    fc2_col_new[...] = col_new.reshape(D)
    update(
        fin.at[1], fc2, to_column(fc_sums[14:15, :], eye), col_new, mean, norm, FF ** (-0.5),
        fc2_grad, fc2_new, fc2_low,
    )

    def stepped(grad, old):
        state = fresh(old, grad * grad)
        return state, grad * lax.rsqrt(state)

    norm = jnp.zeros((1, 1), F32)
    for m in range(4):
        d = (m + 4 - mlp) % 4
        step = stepped(vec[4 + m : 5 + m, :], b1[pl.ds(8 * (d + d // 2 - 2 * (d // 3)) + 4, 1), :])[1]
        norm = norm + jnp.sum(step * step, axis=1, keepdims=True)
    grad = vec[pl.ds(4 + mlp, 1), :]
    state, step = stepped(grad, b1[4:5, :])
    b1_grad[...] = grad.reshape(D)
    b1_state_new[...] = state.reshape(D)
    b1_new[...] = (line(fc1_b[...]) - VEC_RATE * (step * clip_scale(norm * (1.0 / FF)))).reshape(D)

    grad = jnp.concatenate([vec[n : n + 1, :] for n in (20, 21, 22, 23, 0, 1, 2, 3)], axis=1)
    state, step = stepped(grad, line(small_state[...]))
    norm = jnp.sum(step * step, axis=1, keepdims=True) * (1.0 / (8 * D))
    small_grad[...] = grad.reshape(8 * D)
    small_state_new[...] = state.reshape(8 * D)
    small_new[...] = (line(small[...]) - VEC_RATE * (step * clip_scale(norm))).reshape(8 * D)

    grad = vec[8:20, :169]
    state, step = stepped(grad, table_state[...])
    norm = total(step * step) * (1.0 / (169 * HEADS))
    table_grad[...] = grad
    table_state_new[...] = state
    table_new[...] = table[...] - VEC_RATE * (step * clip_scale(norm))
    for _, then in copies:
        then.wait()


def finish(*arrays):
    sd = jax.ShapeDtypeStruct
    vm = pltpu.VMEM
    dma = pltpu.SemaphoreType.DMA

    def owned(width):
        return [sd((3, width), F32), sd((3,), F32), sd((width,), F32), sd((3, width), F32), sd((3, width), BF16)]

    shard = [sd((D, D), F32), sd((D,), F32), sd((D,), F32), sd((D, D), F32), sd((D, D), BF16)]
    out_shape = owned(QKV) + owned(D) + shard + shard
    out_shape += [sd((D,), F32)] * 3 + [sd((8 * D,), F32)] * 3 + [sd((HEADS, 169), F32)] * 3 + [sd((TOK, D), F32)] * 2
    return pl.pallas_call(
        finish_kernel,
        out_shape=out_shape,
        in_specs=[pl.BlockSpec(memory_space=vm)] * 3
        + [pl.BlockSpec(memory_space=pl.ANY)] * 2
        + [pl.BlockSpec(memory_space=vm)] * (len(arrays) - 5),
        out_specs=[pl.BlockSpec(memory_space=vm)] * (len(out_shape) - 2) + [pl.BlockSpec(memory_space=pl.ANY)] * 2,
        scratch_shapes=[vm((2, TOK, D), F32), dma((2, 4)), dma((2, 4))],
        compiler_params=pltpu.CompilerParams(vmem_limit_bytes=63 * 1024 * 1024),
        name="finish",
    )(*arrays)


def clip_scale(mean_square):
    return 1.0 / jnp.maximum(1.0, jnp.sqrt(mean_square))


def per_device(
    tokens_in, out_grad, window_live, region_ids, qkv_weight, proj_weight, rel_table, small_params,
    fc1_weight, fc1_bias, fc2_weight, qkv_row, qkv_col, proj_row, proj_col, fc1_row, fc1_col,
    fc2_row, fc2_col, fc1_bias_state, small_state, table_state,
):
    out, gin, fin, pack = block(
        window_live, region_ids, tokens_in, out_grad, qkv_weight, proj_weight, fc1_weight, fc2_weight, rel_table.T,
        small_params, fc1_bias, fc1_bias_state, fc1_col, fc2_row, qkv_row, proj_row,
    )
    *outs, table_grad, table_state_new, table_new, out, gin = finish(
        fin.reshape(2, D, D), fc1_weight, fc2_weight, out, gin, pack, fc1_bias, fc1_row, fc2_col, qkv_col, proj_col,
        small_params, small_state, rel_table.T, table_state.T,
    )
    return (out, gin, *outs, table_grad.T, table_state_new.T, table_new.T)


def solution(mesh):
    tokens, owner = P(("win", "mlp"), None), P(("win", "mlp"))
    whole, part = P(), P("mlp")
    return jax.shard_map(
        per_device,
        mesh=mesh,
        in_specs=(
            tokens, tokens, owner, owner, whole, whole, whole, whole, P(None, "mlp"), part, P("mlp", None),
            whole, whole, whole, whole, whole, part, part, whole, part, whole, whole,
        ),
        out_specs=(
            tokens, tokens,
            tokens, owner, whole, tokens, tokens,
            tokens, owner, whole, tokens, tokens,
            P(None, "mlp"), whole, part, P(None, "mlp"), P(None, "mlp"),
            P("mlp", None), part, whole, P("mlp", None), P("mlp", None),
            part, part, part,
            whole, whole, whole,
            whole, whole, whole,
        ),
        check_vma=False,
    )
```

profile of v0, /device:TPU:1, one launch (start us, length us, event | category | flops | bytes accessed | tf_op | source)
XLA Modules:
  0.0 96.3 jit_solution(10642008846287367779)
XLA Ops:
  0.7 88.9 %block.1 = (f32[1176,384]{1,0:T(8,128)}, f32[1176,384]{1,0:T(8,128)}, f32[2,4,96,384]{3,2,1,0:T(8,128)}, f32[168,384]{1,0:T(8,128)}) custom-call(s32[24]{0:T(128)} %live_windows.1, s32[1176]{0:T(1024)} %region.1, bf16[1176,384]{1,0:T(8,128)(2,1)} %tok_in.1, bf16[1176,384]{1,0:T(8,128)(2,1)} %og_in.1, f32[384,1152]{1,0:T(8,128)} %wq_in.1, f32[384,384]{1,0:T(8,128)} %wp_in.1, ...), custom_call_target="tpu_custom_call" | custom-call | flops 14000000000 | bytes 20000000 | tf_op jit(solution)/shard_map/block/pallas_call | solution.py:875
  89.5 6.6 %finish.1 = (f32[3,1152]{1,0:T(4,128)}, f32[3]{0:T(128)}, f32[1152]{0:T(1024)}, f32[3,1152]{1,0:T(4,128)}, bf16[3,1152]{1,0:T(4,128)(2,1)}, /*index=5*/f32[3,384...) custom-call(f32[2,384,384]{2,1,0:T(8,128)} %bitcast.6, ...), custom_call_target="tpu_custom_call" | custom-call | tf_op jit(solution)/shard_map/finish/pallas_call | solution.py:1096
where the time goes:
time: 96.5 us; the launch traced here: 96.3 us
  Pallas kernels  95.4 us (99%)
    pallas_call x1, Pallas kernels, block(): pl.pallas_call(block_kernel, out_shape=[sd((TOK, D), F32), sd((TOK, D), F...  88.9 us
    pallas_call x1, Pallas kernels, finish(): pl.pallas_call(finish_kernel, out_shape=out_shape, in_specs=[pl.BlockSpec...  6.59 us

commit v1 on v0

--- a/solution.py
+++ b/solution.py
@@ -351,9 +351,9 @@
         i = iota((CHUNK, 128), 0)
         att[rows, 128 * g : 128 * g + 128] += jnp.where((i >= b) & (i < b + SPAN), collect(full), 0.0)
 
-    @pl.loop(0, 4)
-    def _(pair_at):
-        blocks = [[(a, 2 * pair_at + b, g) for a in range(GROUPS)] for b in range(2) for g in range(SETS)]
+    @pl.loop(0, 2)
+    def _(half):
+        blocks = [[(a, 4 * half + b, g) for a in range(GROUPS)] for b in range(4) for g in range(SETS)]
         ahead = [scores_of(*unit) for unit in blocks[0]]
         for n, units in enumerate(blocks):
             raws = ahead
@@ -388,36 +388,44 @@
             inv2[here, :] = inverse
             n2[here, :] = (scaled * param(5) + param(6)).astype(BF16)
 
-    for nt in range(6):
-        if nt in (1, 3):
+    for tiles in ((0, 1, 2), (3,), (4, 5)):
+        if tiles[0] in (0, 3):
             for n in range(2):
-                across(1 + nt // 2, n).wait_recv()
-        if nt == 3:
+                across(1 + tiles[0] // 3, n).wait_recv()
+        if tiles[0] == 3:
             for n in range(2):
                 far(n).wait_recv()
                 start(across(3, n))
-        if nt == 4:
+        if tiles[0] == 4:
             for n in range(2):
                 across(3, n).wait_recv()
-        cols = slice(256 * nt, 256 * nt + 256)
-        shift = jnp.concatenate(
-            [b1[c // 3, 0:1, 128 * (c % 3) : 128 * (c % 3) + 128] for c in (2 * nt, 2 * nt + 1)], axis=1
-        )
 
         @pl.loop(0, 5)
         def _(mt):
             rows = pl.ds(pl.multiple_of(mt * 240, 16), 240)
-            inner = dot(n2[rows, :], w1[:, cols]) + shift
-            up = dot_nt(back[rows, :], w2[cols, :])
-            total = b1_acc[:, cols]
-            for c in range(15):
-                act, slope = gelu_parts(inner[16 * c : 16 * c + 16])
-                here = pl.ds(pl.multiple_of(mt * 240 + 16 * c, 16), 16)
-                hidden[here, cols] = act.astype(BF16)
-                grad = (up[16 * c : 16 * c + 16] * slope).astype(BF16)
-                ig[here, cols] = grad
-                total = total + fold_rows(grad.astype(F32))
-            b1_acc[:, cols] = total
+
+            def products(nt):
+                cols = slice(256 * nt, 256 * nt + 256)
+                shift = jnp.concatenate(
+                    [b1[c // 3, 0:1, 128 * (c % 3) : 128 * (c % 3) + 128] for c in (2 * nt, 2 * nt + 1)], axis=1
+                )
+                return dot(n2[rows, :], w1[:, cols]) + shift, dot_nt(back[rows, :], w2[cols, :])
+
+            ahead = products(tiles[0])
+            for nt in tiles:
+                inner, up = ahead
+                if nt + 1 in tiles:
+                    ahead = products(nt + 1)
+                cols = slice(256 * nt, 256 * nt + 256)
+                total = b1_acc[:, cols]
+                for c in range(15):
+                    act, slope = gelu_parts(inner[16 * c : 16 * c + 16])
+                    here = pl.ds(pl.multiple_of(mt * 240 + 16 * c, 16), 16)
+                    hidden[here, cols] = act.astype(BF16)
+                    grad = (up[16 * c : 16 * c + 16] * slope).astype(BF16)
+                    ig[here, cols] = grad
+                    total = total + fold_rows(grad.astype(F32))
+                b1_acc[:, cols] = total
 
     g2 = dot_tn(hidden[...], back[...]).astype(BF16)
     g1 = dot_tn(n2[...], ig[...]).astype(BF16)

time: 96.5 us -> 93 us (0.964)
  Pallas kernels: 95.4 us -> 91.9 us
    pallas_call x1, Pallas kernels: 88.9 us -> 85.3 us  [block(): pl.pallas_call(block_kernel, out_shape=[sd((TOK, D), F32), sd((TOK, D), F...]
where the time goes in v1:
time: 93 us; the launch traced here: 92.8 us
  Pallas kernels  91.9 us (99%)
    pallas_call x1, Pallas kernels, block(): pl.pallas_call(block_kernel, out_shape=[sd((TOK, D), F32), sd((TOK, D), F...  85.3 us
    pallas_call x1, Pallas kernels, finish(): pl.pallas_call(finish_kernel, out_shape=out_shape, in_specs=[pl.BlockSpec...  6.59 us

profile of v1, /device:TPU:1, one launch (start us, length us, event | category | flops | bytes accessed | tf_op | source)
XLA Modules:
  0.0 92.8 jit_solution(18355489512641890717)
XLA Ops:
  0.7 85.3 %block.1 = (f32[1176,384]{1,0:T(8,128)}, f32[1176,384]{1,0:T(8,128)}, f32[2,4,96,384]{3,2,1,0:T(8,128)}, f32[168,384]{1,0:T(8,128)}) custom-call(s32[24]{0:T(128)} %live_windows.1, s32[1176]{0:T(1024)} %region.1, bf16[1176,384]{1,0:T(8,128)(2,1)} %tok_in.1, bf16[1176,384]{1,0:T(8,128)(2,1)} %og_in.1, f32[384,1152]{1,0:T(8,128)} %wq_in.1, f32[384,384]{1,0:T(8,128)} %wp_in.1, ...), custom_call_target="tpu_custom_call" | custom-call | flops 14000000000 | bytes 20000000 | tf_op jit(solution)/shard_map/block/pallas_call | solution.py:883
  86.0 6.6 %finish.1 = (f32[3,1152]{1,0:T(4,128)}, f32[3]{0:T(128)}, f32[1152]{0:T(1024)}, f32[3,1152]{1,0:T(4,128)}, bf16[3,1152]{1,0:T(4,128)(2,1)}, /*index=5*/f32[3,384...) custom-call(f32[2,384,384]{2,1,0:T(8,128)} %bitcast.6, ...), custom_call_target="tpu_custom_call" | custom-call | tf_op jit(solution)/shard_map/finish/pallas_call | solution.py:1104
